TPU v7x, 256 devices: a whole 4x4x8 slice. The times are simulated.
256 devices in a mesh: dp: 4 (over x), expert: 8 (over z), etp: 8 (over y, core).
Axes of the slice: x: 4, y: 4, z: 8, core: 2. Of those that a mesh axis runs over, the one named last changes fastest.
Arguments:
- grad_output: bfloat16 [2048, 6144], P(('dp', 'expert', 'etp')), may hold values from -6 to 6
- comb_weights: bfloat16 [2048, 4], P(('dp', 'expert', 'etp')), may hold values from 0.099609375 to 1
- expert_ids: int32 [2048, 4], P(('dp', 'expert', 'etp')), may hold values from 0 to 7, all different within a row; in each aligned block of 8 rows (0 to 7, 8 to 15, ...) at most 6 rows name the same one
- down_weight: bfloat16 [8, 6144, 6144], P('expert', 'etp', 'dp'), may hold values from -0.078125 to 0.078125
- gate_weight: bfloat16 [8, 6144, 6144], P('expert', 'dp', 'etp'), may hold values from -0.078125 to 0.078125
- up_weight: bfloat16 [8, 6144, 6144], P('expert', 'dp', 'etp'), may hold values from -0.078125 to 0.078125
- gate_saved: bfloat16 [8, 1536, 6144], P('expert', None, 'etp'), may hold values from -6 to 6
- up_saved: bfloat16 [8, 1536, 6144], P('expert', None, 'etp'), may hold values from -6 to 6
Outputs:
- input_grad: bfloat16 [2048, 6144], P(('dp', 'expert', 'etp'))
Inputs may be any that keep to these rules, and one draw needn't show every extreme that they name: `expert_ids`: each token names 4 different experts; no expert is named by more than 6 of the tokens of one device.
All inputs are finite; a program needn't handle non-finite values.
Results may differ from a plain program's by a relative error of at most 0.0049.
Values may be sent and summed in bfloat16 or wider, within the bound.
A program may use at most 128 MiB of HBM per device.

v0:
```python
import jax
import jax.numpy as jnp
from jax import lax
from jax.sharding import PartitionSpec as P


def swiglu_backward(hidden_raw, weight, gate_pre, up_pre):
    gate_value = gate_pre.astype(jnp.float32)
    up_value = up_pre.astype(jnp.float32)
    sigmoid_gate = jax.nn.sigmoid(gate_value)
    scaled = hidden_raw * weight[:, None]
    gate_grad = (
        scaled * up_value * sigmoid_gate * (1.0 + gate_value * (1.0 - sigmoid_gate))
    ).astype(jnp.bfloat16)
    up_grad = (scaled * gate_value * sigmoid_gate).astype(jnp.bfloat16)
    return (gate_grad, up_grad)


def on_device(
    grad_output, comb_weights, expert_ids, down_weight, gate_weight, up_weight, gate_saved, up_saved
):
    group_count = lax.axis_size("dp")
    expert_count = lax.axis_size("expert")
    tensor_count = lax.axis_size("etp")
    tokens_here, model_width = grad_output.shape
    choices_count = expert_ids.shape[1]
    capacity = min(
        tokens_here, tokens_here * choices_count // expert_count + max(2, tokens_here // 6)
    )
    quarter = model_width // group_count
    labels = jnp.arange(expert_count, dtype=jnp.int32)
    matches = (expert_ids[:, :, None] == labels[None, None, :]).astype(jnp.int32)
    expert_hits = jnp.sum(matches, axis=1)
    before = jnp.cumsum(expert_hits, axis=0) - expert_hits
    position = jnp.sum(matches * before[:, None, :], axis=2)
    target = expert_ids * capacity + position
    slot_labels = jnp.arange(expert_count * capacity, dtype=jnp.int32)
    chosen = slot_labels[:, None, None] == target[None, :, :]
    selector = (
        jnp.any(chosen, axis=2).astype(jnp.bfloat16).reshape(expert_count, capacity, tokens_here)
    )
    pieces = grad_output.reshape(tokens_here, group_count, quarter)
    outgoing = jnp.einsum(
        "ect,tqd->eqcd", selector, pieces, preferred_element_type=jnp.float32
    ).astype(jnp.bfloat16)
    weight_slots = jnp.sum(
        jnp.where(chosen, comb_weights.astype(jnp.float32)[None, :, :], 0.0), axis=(1, 2)
    )
    weight_out = jnp.broadcast_to(
        weight_slots.reshape(expert_count, 1, capacity), (expert_count, group_count, capacity)
    ).astype(jnp.bfloat16)
    arrived, arrived_weight = (
        lax.all_to_all(outgoing, "dp", split_axis=1, concat_axis=1, tiled=True),
        lax.all_to_all(weight_out, "dp", split_axis=1, concat_axis=1, tiled=True),
    )
    copied = jnp.broadcast_to(
        arrived[:, None], (expert_count, tensor_count, group_count, capacity, quarter)
    )
    copied = copied.reshape(expert_count * tensor_count, group_count, capacity, quarter)
    copied_weight = jnp.broadcast_to(
        arrived_weight[:, None], (expert_count, tensor_count, group_count, capacity)
    )
    copied_weight = copied_weight.reshape(expert_count * tensor_count, group_count, capacity)
    routed, routed_weight = (
        lax.all_to_all(copied, ("expert", "etp"), split_axis=0, concat_axis=0, tiled=True),
        lax.all_to_all(copied_weight, ("expert", "etp"), split_axis=0, concat_axis=0, tiled=True),
    )
    slot_total = expert_count * tensor_count * group_count * capacity
    routed = routed.reshape(slot_total, quarter)
    slot_weight = routed_weight.reshape(slot_total).astype(jnp.float32)
    down_local = down_weight[0]
    gate_local = gate_saved[0]
    up_local = up_saved[0]
    partial_value = jnp.einsum("sq,fq->sf", routed, down_local, preferred_element_type=jnp.float32)
    hidden_raw = lax.psum(partial_value, "dp")
    gate_grad, up_grad = swiglu_backward(hidden_raw, slot_weight, gate_local, up_local)
    slot_grad = jnp.einsum(
        "sf,qf->sq", gate_grad, gate_weight[0], preferred_element_type=jnp.float32
    )
    slot_grad = slot_grad + jnp.einsum(
        "sf,qf->sq", up_grad, up_weight[0], preferred_element_type=jnp.float32
    )
    outbound = slot_grad.reshape(expert_count * tensor_count, group_count, capacity, quarter)
    inbound = lax.all_to_all(outbound, ("expert", "etp"), split_axis=0, concat_axis=0, tiled=True)
    inbound = jnp.sum(
        inbound.reshape(expert_count, tensor_count, group_count, capacity, quarter), axis=1
    )
    complete = lax.all_to_all(inbound, "dp", split_axis=1, concat_axis=3, tiled=True)
    complete = complete.reshape(expert_count * capacity, model_width)
    picked = jnp.take(complete, target.reshape(-1), axis=0)
    picked = picked.reshape(tokens_here, choices_count, model_width)
    return jnp.sum(picked, axis=1).astype(jnp.bfloat16)


def solution(mesh):
    in_specs = (
        P(("dp", "expert", "etp"), None),
        P(("dp", "expert", "etp"), None),
        P(("dp", "expert", "etp"), None),
        P("expert", "etp", "dp"),
        P("expert", "dp", "etp"),
        P("expert", "dp", "etp"),
        P("expert", None, "etp"),
        P("expert", None, "etp"),
    )
    out_specs = P(("dp", "expert", "etp"), None)
    return jax.shard_map(
        on_device, mesh=mesh, in_specs=in_specs, out_specs=out_specs, check_vma=False
    )
```

profile of v0, /device:TPU:32, one launch (start us, length us, event | category | flops | bytes accessed | tf_op | source)
XLA Modules:
  0.0 574.1 jit_solution(5975261550007912184)
XLA Ops:
  6.5 0.9 convert_reduce_fusion
  7.5 0.9 select_reduce_fusion.2
  8.4 0.7 compare_and_fusion
  9.2 0.1 copy.61
  9.4 1.2 fusion.9
  10.6 14.3 %all_to_all.40 = bf16[8,4,6,1536]{3,0,2,1:T(8,128)(2,1)S(1)} all-to-all(bf16[8,4,6,1536]{3,0,2,1:T(8,128)(2,1)S(1)} %copy.52), channel_id=1, replica_groups=mesh['dp'=4,'expert'=8,'etp'=8] {'dp'}, dimensions={1} | all-to-all | bytes 1179648 | tf_op jit(solution)/shard_map/all_to_all | solution.py:53
  24.9 0.5 copy.53
  25.4 1.4 broadcast_in_dim.26
  26.8 118.2 %all_to_all.41 = bf16[64,4,6,1536]{3,1,2,0:T(4,128)(2,1)S(1)} all-to-all(bf16[64,4,6,1536]{3,1,2,0:T(4,128)(2,1)S(1)} %bitcast.46), channel_id=1, replica_groups=mesh['dp'=4,'expert'=8,'etp'=8] {'expert','etp'}, dimensions={0} | all-to-all | bytes 9437184 | tf_op jit(solution)/shard_map/all_to_all | solution.py:65
  145.0 4.4 copy.54
  149.4 8.5 %reshape.100 = bf16[1536,1536]{1,0:T(8,128)(2,1)} reshape(bf16[64,4,6,1536]{3,2,1,0:T(8,128)(2,1)} %copy.54) | data formatting | bytes 9437184 | tf_op jit(solution)/shard_map/reshape | solution.py:69
  157.9 9.2 %fusion.16 = f32[1536,768]{1,0:T(8,128)} fusion(bf16[1536,1536]{1,0:T(8,128)(2,1)} %reshape.100, bf16[1,768,1536]{2,1,0:T(8,128)(2,1)} %param.11), kind=kOutput, calls=%fused_computation.22 | convolution fusion | flops 3623878656 | bytes 11796480 | tf_op jit(solution)/shard_map/sq,fq->sf/dot_general | solution.py:74
  167.1 0.7 copy-done.2
  167.7 0.1 select_reduce_fusion.1
  167.9 7.6 %all_to_all.42 = bf16[8,4,6]{2,0,1:T(8,128)(2,1)S(1)} all-to-all(bf16[8,4,6]{2,0,1:T(8,128)(2,1)S(1)} %broadcast_in_dim.50), channel_id=1, replica_groups=mesh['dp'=4,'expert'=8,'etp'=8] {'dp'}, dimensions={1} | all-to-all | bytes 768 | tf_op jit(solution)/shard_map/all_to_all | solution.py:54
  175.6 15.6 %all_to_all.43 = bf16[64,4,6]{2,1,0:T(4,128)(2,1)S(1)} all-to-all(bf16[64,4,6]{2,1,0:T(4,128)(2,1)S(1)} %bitcast.49), channel_id=1, replica_groups=mesh['dp'=4,'expert'=8,'etp'=8] {'expert','etp'}, dimensions={0} | all-to-all | bytes 6144 | tf_op jit(solution)/shard_map/all_to_all | solution.py:66
  191.2 0.1 reshape.106
  191.4 78.0 %all-reduce.2.cloned.1.call-done = f32[1536,768]{1,0:T(8,128)} async-done(((f32[1536,768]{1,0:T(8,128)}), f32[1536,768]{1,0:T(8,128)}) %all-reduce.2.cloned.1.call-update) | async-done | bytes 4718608 | tf_op jit(solution)/shard_map/psum | solution.py:75
  269.4 12.6 %fusion.12 = f32[1536,1536]{1,0:T(8,128)} fusion(bf16[1,1536,768]{2,1,0:T(8,128)(2,1)S(1)} %copy-done, f32[1536,768]{1,0:T(8,128)} %all-reduce.2.cloned.1.call-done, bf16[1,1536,768]{2,1,0:T(8,128)(2,1)} %param.15, bf16[1,1536,768]{2,1,0:T(8,128)(2,1)} %param.14, f32[1536]{0:T(1024)S(1)} %reshape.106), kind=kOutput, calls=%fused_computation.19 | convolution fusion | flops 3639214080 | bytes 21239808 | tf_op jit(solution)/shard_map/sf,qf->sq/dot_general | solution.py:77
  281.9 9.5 %convolution_add_fusion = f32[1536,1536]{1,0:T(8,128)} fusion(f32[1536,1536]{1,0:T(8,128)} %fusion.12, f32[1536,768]{1,0:T(8,128)S(1)} %copy-done.3, bf16[1,1536,768]{2,1,0:T(8,128)(2,1)S(1)} %copy-done.5, bf16[1,1536,768]{2,1,0:T(8,128)(2,1)S(1)} %copy-done.4, f32[1536]{0:T(1024)S(1)} %reshape.106), kind=kOutput, calls=%fused_computation.2 | convolution fusion | flops 3635675136 | bytes 28317696 | tf_op jit(solution)/shard_map/sf,qf->sq/dot_general | solution.py:80
  291.4 11.4 %reshape.102 = f32[64,4,6,1536]{3,2,1,0:T(8,128)} reshape(f32[1536,1536]{1,0:T(8,128)} %convolution_add_fusion) | data formatting | bytes 18874368 | tf_op jit(solution)/shard_map/reshape | solution.py:83
  302.8 17.0 %copy.56 = f32[64,4,6,1536]{3,1,2,0:T(4,128)} copy(f32[64,4,6,1536]{3,2,1,0:T(8,128)} %reshape.102) | data formatting | bytes 18874368 | tf_op jit(solution)/shard_map/reshape | solution.py:83
  319.8 218.2 %all_to_all.44 = f32[64,4,6,1536]{3,1,2,0:T(4,128)S(1)} all-to-all(f32[64,4,6,1536]{3,1,2,0:T(4,128)} %copy.56), channel_id=1, replica_groups=mesh['dp'=4,'expert'=8,'etp'=8] {'expert','etp'}, dimensions={0} | all-to-all | bytes 18874368 | tf_op jit(solution)/shard_map/all_to_all | solution.py:84
  537.9 1.5 bitcast_reduce_fusion
  539.4 1.7 copy.58
  541.1 3.5 all-to-all-start.5
  544.9 16.9 %all-to-all-done.5 = f32[8,4,6,1536]{3,0,2,1:T(8,128)S(1)} async-done(((f32[8,4,6,1536]{3,0,2,1:T(8,128)}), f32[8,4,6,1536]{3,0,2,1:T(8,128)S(1)}, u32[]{:S(2)}, u32[]{:S(2)}) %all-to-all-start.5) | async-done | bytes 1179680 | tf_op jit(solution)/shard_map/all_to_all | solution.py:88
  561.8 0.8 copy.59
  562.6 0.4 copy.66
  563.0 1.7 gather_fusion
  564.6 1.4 gather.7
  566.0 1.2 select_reduce_fusion
  (28 shorter events, 0.7 us)
Async XLA Ops:
  6.5 262.8 %copy-start = (bf16[1,1536,768]{2,1,0:T(8,128)(2,1)S(1)}, bf16[1,1536,768]{2,1,0:T(8,128)(2,1)}, u32[]{:S(2)}) copy-start(bf16[1,1536,768]{2,1,0:T(8,128)(2,1)} %param.12) | copy-start | bytes 7077892
  6.5 262.8 %all-reduce.2.cloned.1.call-start = ((), (), s32[]{:S(2)}) async-start(), calls=%async_computation.6 | async-start | bytes 9437184 | tf_op jit(solution)/shard_map/psum | solution.py:75
  167.0 0.7 copy-start.2
  269.3 12.6 %copy-start.3 = (f32[1536,768]{1,0:T(8,128)S(1)}, f32[1536,768]{1,0:T(8,128)}, u32[]{:S(2)}) copy-start(f32[1536,768]{1,0:T(8,128)} %all-reduce.2.cloned.1.call-done) | copy-start | bytes 14155780
  269.3 12.6 %copy-start.4 = (bf16[1,1536,768]{2,1,0:T(8,128)(2,1)S(1)}, bf16[1,1536,768]{2,1,0:T(8,128)(2,1)}, u32[]{:S(2)}) copy-start(bf16[1,1536,768]{2,1,0:T(8,128)(2,1)} %param.14) | copy-start | bytes 7077892
  269.3 12.6 %copy-start.5 = (bf16[1,1536,768]{2,1,0:T(8,128)(2,1)S(1)}, bf16[1,1536,768]{2,1,0:T(8,128)(2,1)}, u32[]{:S(2)}) copy-start(bf16[1,1536,768]{2,1,0:T(8,128)(2,1)} %param.13) | copy-start | bytes 7077892
  541.1 20.7 %all-to-all-start.5 = ((f32[8,4,6,1536]{3,0,2,1:T(8,128)}), f32[8,4,6,1536]{3,0,2,1:T(8,128)S(1)}, u32[]{:S(2)}, u32[]{:S(2)}) async-start(f32[8,4,6,1536]{3,0,2,1:T(8,128)} %copy.58), calls=%async_computation.5 | async-start | bytes 2359296 | tf_op jit(solution)/shard_map/all_to_all | solution.py:88
  563.0 4.3 copy-start.1
Sparse Core Ops, SparseCore 0:
  167.2 102.1 all-reduce.1
where the time goes:
time: 575 us; the launch traced here: 574 us
  blocking collectives  374 us (65%)
  waiting for transfers between devices  94.9 us (17%)
  local copies, waits for them, and re-layouts  50.4 us (9%)
  matrix products  32.4 us (6%)
  between operations  13.5 us (2%)
    all_to_all x1, blocking collectives, on_device(): lax.all_to_all(outbound, ('expert', 'etp'), split_axis=0, concat_axis=0,...  218 us
    all_to_all x1, blocking collectives, on_device(): lax.all_to_all(copied, ('expert', 'etp'), split_axis=0, concat_axis=0, ti...  118 us
    psum x1, waiting for transfers between devices, on_device(): hidden_raw = lax.psum(partial_value, 'dp')  78 us
    reshape x2, local copies, waits for them, and re-layouts, on_device(): slot_grad.reshape(expert_count * tensor_count, group_count, capacity, qua...  28.4 us
    all_to_all x1, waiting for transfers between devices, on_device(): lax.all_to_all(inbound, 'dp', split_axis=1, concat_axis=3, tiled=True)  16.9 us
    all_to_all x1, blocking collectives, on_device(): lax.all_to_all(copied_weight, ('expert', 'etp'), split_axis=0, concat_axi...  15.6 us
    all_to_all x1, blocking collectives, on_device(): lax.all_to_all(outgoing, 'dp', split_axis=1, concat_axis=1, tiled=True)  14.3 us
    dot_general x1, matrix products, on_device(): jnp.einsum('sf,qf->sq', gate_grad, gate_weight[0], preferred_element_type...  12.6 us
  transfers between devices with their start and end apart: 2, of which 2 were waited for; matrix products, arithmetic and copies ran while one was open for 0% of the time, Pallas kernels for 0%

commit v1 on v0

--- a/solution.py
+++ b/solution.py
@@ -72,7 +72,7 @@
     gate_local = gate_saved[0]
     up_local = up_saved[0]
     partial_value = jnp.einsum("sq,fq->sf", routed, down_local, preferred_element_type=jnp.float32)
-    hidden_raw = lax.psum(partial_value, "dp")
+    hidden_raw = jnp.sum(lax.all_gather(partial_value, "dp"), axis=0)
     gate_grad, up_grad = swiglu_backward(hidden_raw, slot_weight, gate_local, up_local)
     slot_grad = jnp.einsum(
         "sf,qf->sq", gate_grad, gate_weight[0], preferred_element_type=jnp.float32

time: 575 us -> 654 us (1.14)
  waiting for transfers between devices: 94.9 us -> 163 us
  other arithmetic: 5.45 us -> 15.8 us
    all_gather x0 -> x1, waiting for transfers between devices: none -> 147 us  [on_device(): hidden_raw = jnp.sum(lax.all_gather(partial_value, 'dp'), axis=0)]
    psum x1 -> x0, waiting for transfers between devices: 78 us -> none  [on_device(): hidden_raw = lax.psum(partial_value, 'dp')]
    reduce_sum x0 -> x1, other arithmetic: none -> 10.4 us  [on_device(): hidden_raw = jnp.sum(lax.all_gather(partial_value, 'dp'), axis=0)]
where the time goes in v1:
time: 654 us; the launch traced here: 653 us
  blocking collectives  374 us (57%)
  waiting for transfers between devices  163 us (25%)
  local copies, waits for them, and re-layouts  50.5 us (8%)
  matrix products  32.4 us (5%)
  other arithmetic  15.8 us (2%)
  between operations  13.5 us (2%)
    all_to_all x1, blocking collectives, on_device(): lax.all_to_all(outbound, ('expert', 'etp'), split_axis=0, concat_axis=0,...  218 us
    all_gather x1, waiting for transfers between devices, on_device(): hidden_raw = jnp.sum(lax.all_gather(partial_value, 'dp'), axis=0)  147 us
    all_to_all x1, blocking collectives, on_device(): lax.all_to_all(copied, ('expert', 'etp'), split_axis=0, concat_axis=0, ti...  118 us
    reshape x2, local copies, waits for them, and re-layouts, on_device(): slot_grad.reshape(expert_count * tensor_count, group_count, capacity, qua...  28.5 us
    all_to_all x1, waiting for transfers between devices, on_device(): lax.all_to_all(inbound, 'dp', split_axis=1, concat_axis=3, tiled=True)  16.9 us
    all_to_all x1, blocking collectives, on_device(): lax.all_to_all(copied_weight, ('expert', 'etp'), split_axis=0, concat_axi...  15.6 us
    all_to_all x1, blocking collectives, on_device(): lax.all_to_all(outgoing, 'dp', split_axis=1, concat_axis=1, tiled=True)  14.3 us
  transfers between devices with their start and end apart: 2, of which 2 were waited for; matrix products, arithmetic and copies ran while one was open for 0% of the time, Pallas kernels for 0%

profile of v1, /device:TPU:32, one launch (start us, length us, event | category | flops | bytes accessed | tf_op | source)
XLA Modules:
  0.0 653.1 jit_solution(11724085955026843318)
XLA Ops:
  6.5 0.9 convert_reduce_fusion
  7.5 0.9 select_reduce_fusion.2
  8.4 0.7 compare_and_fusion
  9.2 0.1 copy.61
  9.4 1.2 fusion.8
  10.6 14.3 %all_to_all.40 = bf16[8,4,6,1536]{3,0,2,1:T(8,128)(2,1)S(1)} all-to-all(bf16[8,4,6,1536]{3,0,2,1:T(8,128)(2,1)S(1)} %copy.52), channel_id=1, replica_groups=mesh['dp'=4,'expert'=8,'etp'=8] {'dp'}, dimensions={1} | all-to-all | bytes 1179648 | tf_op jit(solution)/shard_map/all_to_all | solution.py:53
  24.9 0.5 copy.53
  25.4 1.4 broadcast_in_dim.26
  26.8 118.2 %all_to_all.41 = bf16[64,4,6,1536]{3,1,2,0:T(4,128)(2,1)S(1)} all-to-all(bf16[64,4,6,1536]{3,1,2,0:T(4,128)(2,1)S(1)} %bitcast.54), channel_id=1, replica_groups=mesh['dp'=4,'expert'=8,'etp'=8] {'expert','etp'}, dimensions={0} | all-to-all | bytes 9437184 | tf_op jit(solution)/shard_map/all_to_all | solution.py:65
  145.0 4.5 copy.54
  149.4 8.4 %reshape.132 = bf16[1536,1536]{1,0:T(8,128)(2,1)} reshape(bf16[64,4,6,1536]{3,2,1,0:T(8,128)(2,1)} %copy.54) | data formatting | bytes 9437184 | tf_op jit(solution)/shard_map/reshape | solution.py:69
  157.8 9.1 %fusion.14 = f32[1536,768]{1,0:T(8,128)} fusion(bf16[1536,1536]{1,0:T(8,128)(2,1)} %reshape.132, bf16[1,768,1536]{2,1,0:T(8,128)(2,1)} %param.11), kind=kOutput, calls=%fused_computation.22 | convolution fusion | flops 3623878656 | bytes 11796480 | tf_op jit(solution)/shard_map/sq,fq->sf/dot_general | solution.py:74
  167.0 0.7 copy-done.3
  167.9 7.6 %all_to_all.42 = bf16[8,4,6]{2,0,1:T(8,128)(2,1)S(1)} all-to-all(bf16[8,4,6]{2,0,1:T(8,128)(2,1)S(1)} %broadcast_in_dim.50), channel_id=1, replica_groups=mesh['dp'=4,'expert'=8,'etp'=8] {'dp'}, dimensions={1} | all-to-all | bytes 768 | tf_op jit(solution)/shard_map/all_to_all | solution.py:54
  175.5 15.6 %all_to_all.43 = bf16[64,4,6]{2,1,0:T(4,128)(2,1)S(1)} all-to-all(bf16[64,4,6]{2,1,0:T(4,128)(2,1)S(1)} %bitcast.57), channel_id=1, replica_groups=mesh['dp'=4,'expert'=8,'etp'=8] {'expert','etp'}, dimensions={0} | all-to-all | bytes 6144 | tf_op jit(solution)/shard_map/all_to_all | solution.py:66
  191.2 0.1 reshape.138
  191.3 146.5 %all-gather.3.cloned.1.call-done = f32[6144,768]{1,0:T(8,128)} async-done(((f32[1536,768]{1,0:T(8,128)}), f32[6144,768]{1,0:T(8,128)}) %all-gather.3.cloned.1.call-update) | async-done | bytes 18874384 | tf_op jit(solution)/shard_map/all_gather | solution.py:75
  337.8 10.4 %reduce_sum.58 = f32[1536,768]{1,0:T(8,128)} reduce(f32[4,1536,768]{2,1,0:T(8,128)} %bitcast.53, f32[]{:T(128)} %constant.26.clone.1), dimensions={0}, to_apply=%region_4.5 | reduce | flops 3538944 | bytes 23592964 | tf_op jit(solution)/shard_map/reduce_sum | solution.py:75
  348.2 12.7 %fusion.11 = f32[1536,1536]{1,0:T(8,128)} fusion(bf16[1,1536,768]{2,1,0:T(8,128)(2,1)S(1)} %copy-done, bf16[1,1536,768]{2,1,0:T(8,128)(2,1)} %param.14, bf16[1,1536,768]{2,1,0:T(8,128)(2,1)} %param.15, f32[1536,768]{1,0:T(8,128)} %reduce_sum.58, f32[1536]{0:T(1024)S(1)} %reshape.138), kind=kOutput, calls=%fused_computation.19 | convolution fusion | flops 3639214080 | bytes 21239808 | tf_op jit(solution)/shard_map/sf,qf->sq/dot_general | solution.py:77
  360.9 9.5 %convolution_add_fusion = f32[1536,1536]{1,0:T(8,128)} fusion(f32[1536,1536]{1,0:T(8,128)} %fusion.11, bf16[1,1536,768]{2,1,0:T(8,128)(2,1)S(1)} %copy-done.5, bf16[1,1536,768]{2,1,0:T(8,128)(2,1)S(1)} %copy-done.4, f32[1536,768]{1,0:T(8,128)S(1)} %copy-done.2, f32[1536]{0:T(1024)S(1)} %reshape.138), kind=kOutput, calls=%fused_computation.2 | convolution fusion | flops 3635675136 | bytes 28317696 | tf_op jit(solution)/shard_map/sf,qf->sq/dot_general | solution.py:80
  370.3 11.4 %reshape.134 = f32[64,4,6,1536]{3,2,1,0:T(8,128)} reshape(f32[1536,1536]{1,0:T(8,128)} %convolution_add_fusion) | data formatting | bytes 18874368 | tf_op jit(solution)/shard_map/reshape | solution.py:83
  381.8 17.0 %copy.56 = f32[64,4,6,1536]{3,1,2,0:T(4,128)} copy(f32[64,4,6,1536]{3,2,1,0:T(8,128)} %reshape.134) | data formatting | bytes 18874368 | tf_op jit(solution)/shard_map/reshape | solution.py:83
  398.8 218.2 %all_to_all.44 = f32[64,4,6,1536]{3,1,2,0:T(4,128)S(1)} all-to-all(f32[64,4,6,1536]{3,1,2,0:T(4,128)} %copy.56), channel_id=1, replica_groups=mesh['dp'=4,'expert'=8,'etp'=8] {'expert','etp'}, dimensions={0} | all-to-all | bytes 18874368 | tf_op jit(solution)/shard_map/all_to_all | solution.py:84
  617.0 1.5 bitcast_reduce_fusion
  618.5 1.7 copy.58
  620.2 3.5 all-to-all-start.5
  624.0 16.9 %all-to-all-done.5 = f32[8,4,6,1536]{3,0,2,1:T(8,128)S(1)} async-done(((f32[8,4,6,1536]{3,0,2,1:T(8,128)}), f32[8,4,6,1536]{3,0,2,1:T(8,128)S(1)}, u32[]{:S(2)}, u32[]{:S(2)}) %all-to-all-start.5) | async-done | bytes 1179680 | tf_op jit(solution)/shard_map/all_to_all | solution.py:88
  640.9 0.8 copy.59
  641.6 0.4 copy.66
  642.0 1.7 gather_fusion
  643.7 1.4 gather.7
  645.1 1.2 select_reduce_fusion
  (29 shorter events, 0.8 us)
Async XLA Ops:
  6.5 341.7 %copy-start = (bf16[1,1536,768]{2,1,0:T(8,128)(2,1)S(1)}, bf16[1,1536,768]{2,1,0:T(8,128)(2,1)}, u32[]{:S(2)}) copy-start(bf16[1,1536,768]{2,1,0:T(8,128)(2,1)} %param.12) | copy-start | bytes 7077892
  6.5 331.3 %all-gather.3.cloned.1.call-start = ((), (), s32[]{:S(2)}) async-start(), calls=%async_computation.6 | async-start | bytes 23592960 | tf_op jit(solution)/shard_map/all_gather | solution.py:75
  167.0 0.7 copy-start.3
  348.2 12.7 %copy-start.2 = (f32[1536,768]{1,0:T(8,128)S(1)}, f32[1536,768]{1,0:T(8,128)}, u32[]{:S(2)}) copy-start(f32[1536,768]{1,0:T(8,128)} %reduce_sum.58) | copy-start | bytes 14155780
  348.2 12.7 %copy-start.4 = (bf16[1,1536,768]{2,1,0:T(8,128)(2,1)S(1)}, bf16[1,1536,768]{2,1,0:T(8,128)(2,1)}, u32[]{:S(2)}) copy-start(bf16[1,1536,768]{2,1,0:T(8,128)(2,1)} %param.14) | copy-start | bytes 7077892
  348.2 12.7 %copy-start.5 = (bf16[1,1536,768]{2,1,0:T(8,128)(2,1)S(1)}, bf16[1,1536,768]{2,1,0:T(8,128)(2,1)}, u32[]{:S(2)}) copy-start(bf16[1,1536,768]{2,1,0:T(8,128)(2,1)} %param.13) | copy-start | bytes 7077892
  620.2 20.7 %all-to-all-start.5 = ((f32[8,4,6,1536]{3,0,2,1:T(8,128)}), f32[8,4,6,1536]{3,0,2,1:T(8,128)S(1)}, u32[]{:S(2)}, u32[]{:S(2)}) async-start(f32[8,4,6,1536]{3,0,2,1:T(8,128)} %copy.58), calls=%async_computation.5 | async-start | bytes 2359296 | tf_op jit(solution)/shard_map/all_to_all | solution.py:88
  642.0 4.3 copy-start.1
Sparse Core Ops, SparseCore 0:
  167.1 170.6 all-gather.2
